TPU v7x, 32 devices: a whole 2x2x4 slice. The times are simulated.
32 devices in a mesh: img: 4 (over y, x), ch: 8 (over z, core).
Axes of the slice: x: 2, y: 2, z: 4, core: 2. Of those that a mesh axis runs over, the one named last changes fastest.
Arguments:
- images_in: bfloat16 [256, 49, 2048], P('img'), may hold values from -6 to 6
- labels: int32 [256], P(('img', 'ch')), may hold values from 0 to 999
- loss_wt: int32 [256], P(('img', 'ch')), may hold values from 1 to 32
- placement: int32 [4, 64], P('img'), may hold values from 0 to 63, each once within a row
- w_one: float32 [2048, 512], P(None, 'ch'), may hold values from -0.125 to 0.125
- mom_one: float32 [2048, 512], P(None, 'ch'), may hold values from -0.0029296875 to 0.0029296875
- avg_one: float32 [2048, 512], P(None, 'ch'), may hold values from -0.125 to 0.125
- mask_one: int32 [2048, 512], P(None, 'ch'), may hold values 0 or 1
- rank_one: int32 [2048, 512], P(None, 'ch'), may hold values from 0 to 99
- first_norm_params: float32 [2, 512], P(None, 'ch'), may hold values from 0.5 to 1.5
- mom_bn_one: float32 [2, 512], P(None, 'ch'), may hold values from -0.001953125 to 0.001953125
- avg_bn_one: float32 [2, 512], P(None, 'ch'), may hold values from 0.5 to 1.5
- w_two: float32 [2359296], P(('img', 'ch')), may hold values from -0.09375 to 0.09375
- mom_two: float32 [2359296], P(('img', 'ch')), may hold values from -0.01171875 to 0.01171875
- avg_two: float32 [2359296], P(('img', 'ch')), may hold values from -0.09375 to 0.09375
- mask_two: int32 [2359296], P(('img', 'ch')), may hold values 0 or 1
- rank_two: int32 [2359296], P(('img', 'ch')), may hold values from 0 to 99
- second_norm_params: float32 [2, 512], replicated, may hold values from 0.5 to 1.5
- mom_bn_two: float32 [2, 512], replicated, may hold values from -0.01953125 to 0.01953125
- avg_bn_two: float32 [2, 512], replicated, may hold values from 0.5 to 1.5
- w_head: float32 [512000], P(('img', 'ch')), may hold values from -0.75 to 0.75
- mom_head: float32 [512000], P(('img', 'ch')), may hold values from -0.0029296875 to 0.0029296875
- avg_head: float32 [512000], P(('img', 'ch')), may hold values from -0.75 to 0.75
Outputs:
- loss: float32 [], replicated
- new_w_one: float32 [2048, 512], P(None, 'ch')
- new_mom_one: float32 [2048, 512], P(None, 'ch')
- new_avg_one: float32 [2048, 512], P(None, 'ch')
- new_mask_one: int32 [2048, 512], P(None, 'ch')
- copy_w_one: bfloat16 [2048, 512], P(None, 'ch')
- new_bn_one: float32 [2, 512], P(None, 'ch')
- new_mom_bn_one: float32 [2, 512], P(None, 'ch')
- new_avg_bn_one: float32 [2, 512], P(None, 'ch')
- new_w_two: float32 [2359296], P(('img', 'ch'))
- new_mom_two: float32 [2359296], P(('img', 'ch'))
- new_avg_two: float32 [2359296], P(('img', 'ch'))
- new_mask_two: int32 [2359296], P(('img', 'ch'))
- copy_w_two: bfloat16 [2359296], P(('img', 'ch'))
- new_bn_two: float32 [2, 512], replicated
- new_mom_bn_two: float32 [2, 512], replicated
- new_avg_bn_two: float32 [2, 512], replicated
- new_w_head: float32 [512000], P(('img', 'ch'))
- new_mom_head: float32 [512000], P(('img', 'ch'))
- new_avg_head: float32 [512000], P(('img', 'ch'))
- copy_w_head: bfloat16 [512000], P(('img', 'ch'))
Inputs may be any that keep to these rules, and one draw needn't show every extreme that they name: `placement`: each row is a permutation of 0 to 63.
All inputs are finite; a program needn't handle non-finite values. No bound on the sum of `mask_one` or of `mask_two` on one device may be relied on, other than what follows from the above.
Results may differ from a plain program's by a relative error of at most 0.013.
Values may be sent and summed in bfloat16 or wider, within the bound.
A program may use at most 512 MiB of HBM per device.

v0:
```python
import math
import jax
import jax.numpy as jnp
from jax import lax
from jax.sharding import PartitionSpec as P

SIDE = 7
PIX = 49
DROP = 10
GROW = 10
EPS = 1e-05
MOMENTUM = 0.5


def advance(weight, grad, velocity, rate):
    velocity = MOMENTUM * velocity + grad
    return (weight - rate * (grad + MOMENTUM * velocity), velocity)


def dense_update(weight, grad, velocity, average, rate):
    moved, velocity = advance(weight, grad, velocity, rate)
    return (moved, velocity, 0.5 * average + 0.5 * moved)


def sparse_update(weight, grad, velocity, average, mask, rank, rate):
    moved, velocity = advance(weight, grad, velocity, rate)
    kept = (mask == 1) & (rank >= DROP)
    grown = (mask == 0) & (rank < GROW)
    new_mask = jnp.where(kept | grown, 1, 0).astype(jnp.int32)
    weight = jnp.where(kept, moved, 0.0)
    velocity = jnp.where(kept, velocity, 0.0)
    average = 0.5 * average + 0.5 * weight
    return (weight, velocity, average, new_mask, weight.astype(jnp.bfloat16))


def silu_slope(value):
    sigma = jax.nn.sigmoid(value)
    return sigma * (1.0 + value * (1.0 - sigma))


def apply_batch_norm(z, sums, squares, element_count):
    mean = sums / element_count
    inverse_deviation = lax.rsqrt(squares / element_count - mean * mean + EPS)
    return ((z - mean) * inverse_deviation, inverse_deviation)


def batch_norm_backward(
    norm_gain,
    inverse_deviation,
    output_gradient,
    standardized_input,
    bias_gradient_sum,
    gain_gradient_sum,
    element_count,
):
    return (
        norm_gain
        * inverse_deviation
        * (
            output_gradient
            - bias_gradient_sum / element_count
            - standardized_input * gain_gradient_sum / element_count
        )
    )


def contract_rows(left, right):
    return jnp.einsum("pk,pc->kc", left, right, preferred_element_type=jnp.float32)


def shards(
    images_in,
    labels,
    loss_wt,
    placement,
    w_one,
    mom_one,
    avg_one,
    mask_one,
    rank_one,
    first_norm_params,
    mom_bn_one,
    avg_bn_one,
    w_two,
    mom_two,
    avg_two,
    mask_two,
    rank_two,
    second_norm_params,
    mom_bn_two,
    avg_bn_two,
    w_head,
    mom_head,
    avg_head,
):
    n_img = lax.axis_size("img")
    n_ch = lax.axis_size("ch")
    group = images_in.shape[0]
    element_count = labels.shape[0]
    width = second_norm_params.shape[1]
    classes = w_head.shape[0] * n_img * n_ch // width
    images = element_count * n_img * n_ch
    slot_info = jnp.stack([labels.astype(jnp.float32), loss_wt.astype(jnp.float32)])
    slot_info = lax.all_gather(slot_info, "ch", axis=1, tiled=True)
    own = lax.axis_index("ch") * element_count + jnp.arange(element_count, dtype=jnp.int32)
    fills = placement[0][None, :] == own[:, None]
    labels_f, weights = jnp.sum(jnp.where(fills[None], slot_info[:, None, :], 0.0), axis=2)
    labels = labels_f.astype(jnp.int32)
    kernel_part = (w_two * mask_two.astype(jnp.float32)).astype(jnp.bfloat16)
    kernel = lax.all_gather(kernel_part, ("img", "ch"), axis=0, tiled=True)
    head = lax.all_gather(w_head.astype(jnp.bfloat16), ("img", "ch"), axis=0, tiled=True)
    kernel = kernel.reshape(9 * width, width)
    head = head.reshape(width, classes)
    rows = images_in.transpose(1, 0, 2).reshape(PIX * group, images_in.shape[2])
    filt_one = (w_one * mask_one.astype(jnp.float32)).astype(jnp.bfloat16)
    first_conv_output = jnp.dot(rows, filt_one, preferred_element_type=jnp.float32)
    first_feature_sum, first_squares_sum, total = lax.psum(
        (
            jnp.sum(first_conv_output, axis=0),
            jnp.sum(first_conv_output * first_conv_output, axis=0),
            jnp.sum(slot_info[1]),
        ),
        "img",
    )
    first_element_count = group * PIX * n_img
    first_standardized_input, first_inverse_deviation = apply_batch_norm(
        first_conv_output, first_feature_sum, first_squares_sum, first_element_count
    )
    first_norm_output = first_norm_params[0] * first_standardized_input + first_norm_params[1]
    act = jax.nn.silu(first_norm_output).astype(jnp.bfloat16).reshape(PIX, group, -1)
    act_in = lax.all_to_all(act, "ch", split_axis=1, concat_axis=2, tiled=True)
    padded = jnp.pad(
        act_in.reshape(SIDE, SIDE, element_count, width), ((1, 1), (1, 1), (0, 0), (0, 0))
    )
    patches = jnp.concatenate(
        [
            padded[tap // 3 : tap // 3 + SIDE, tap % 3 : tap % 3 + SIDE].reshape(
                PIX * element_count, width
            )
            for tap in range(9)
        ],
        axis=1,
    )
    second_conv_output = jnp.dot(patches, kernel, preferred_element_type=jnp.float32)
    second_feature_sum, second_squares_sum = lax.psum(
        (
            jnp.sum(second_conv_output, axis=0),
            jnp.sum(second_conv_output * second_conv_output, axis=0),
        ),
        ("img", "ch"),
    )
    second_element_count = images * PIX
    second_standardized_input, second_inverse_deviation = apply_batch_norm(
        second_conv_output, second_feature_sum, second_squares_sum, second_element_count
    )
    second_norm_output = second_norm_params[0] * second_standardized_input + second_norm_params[1]
    pooled = jnp.mean(jax.nn.silu(second_norm_output).reshape(PIX, element_count, width), axis=0)
    pooled_low = pooled.astype(jnp.bfloat16)
    logits = jnp.dot(pooled_low, head, preferred_element_type=jnp.float32)
    top = jnp.max(logits, axis=1, keepdims=True)
    expd = jnp.exp(logits - top)
    denom = jnp.sum(expd, axis=1, keepdims=True)
    lse = top[:, 0] + jnp.log(denom[:, 0])
    onehot = labels[:, None] == jnp.arange(classes, dtype=jnp.int32)[None, :]
    picked = jnp.sum(jnp.where(onehot, logits, 0.0), axis=1)
    share = weights / total
    partial_loss_value = jnp.sum(share * (lse - picked))
    d_logits = (share[:, None] * (expd / denom - onehot.astype(jnp.float32))).astype(jnp.bfloat16)
    g_head = contract_rows(pooled_low, d_logits)
    d_pooled = jnp.einsum("ic,kc->ik", d_logits, head, preferred_element_type=jnp.float32)
    d_act = jnp.broadcast_to(d_pooled[None] / PIX, (PIX, element_count, width)).reshape(
        PIX * element_count, width
    )
    second_output_gradient = d_act * silu_slope(second_norm_output)
    second_shift_bias, second_norm_gain, loss = lax.psum(
        (
            jnp.sum(second_output_gradient, axis=0),
            jnp.sum(second_output_gradient * second_standardized_input, axis=0),
            partial_loss_value,
        ),
        ("img", "ch"),
    )
    second_preact_gradient = batch_norm_backward(
        second_norm_params[0],
        second_inverse_deviation,
        second_output_gradient,
        second_standardized_input,
        second_shift_bias,
        second_norm_gain,
        second_element_count,
    ).astype(jnp.bfloat16)
    d_patches = jnp.einsum(
        "pc,kc->pk", second_preact_gradient, kernel, preferred_element_type=jnp.float32
    )
    d_pad = 0.0
    for tap in range(9):
        piece = d_patches[:, tap * width : (tap + 1) * width].reshape(
            SIDE, SIDE, element_count, width
        )
        up, left = (tap // 3, tap % 3)
        d_pad = d_pad + jnp.pad(piece, ((up, 2 - up), (left, 2 - left), (0, 0), (0, 0)))
    d_act_in = d_pad[1:-1, 1:-1].astype(jnp.bfloat16).reshape(PIX, element_count, width)
    d_act_one = lax.all_to_all(d_act_in, "ch", split_axis=2, concat_axis=1, tiled=True)
    g_kernel = contract_rows(patches, second_preact_gradient)
    d_act_one = d_act_one.reshape(PIX * group, -1).astype(jnp.float32)
    first_output_gradient = d_act_one * silu_slope(first_norm_output)
    first_shift_bias, first_norm_gain = lax.psum(
        (
            jnp.sum(first_output_gradient, axis=0),
            jnp.sum(first_output_gradient * first_standardized_input, axis=0),
        ),
        "img",
    )
    first_preact_gradient = batch_norm_backward(
        first_norm_params[0],
        first_inverse_deviation,
        first_output_gradient,
        first_standardized_input,
        first_shift_bias,
        first_norm_gain,
        first_element_count,
    ).astype(jnp.bfloat16)
    g_filt = lax.psum(
        contract_rows(rows, first_preact_gradient).astype(jnp.bfloat16), "img"
    ).astype(jnp.float32)
    g_one = g_filt * mask_one.astype(jnp.float32)
    part_two = lax.psum_scatter(g_kernel.reshape(-1), ("img", "ch"), tiled=True)
    part_head = lax.psum_scatter(g_head.reshape(-1), ("img", "ch"), tiled=True)
    g_two = part_two * mask_two.astype(jnp.float32)
    root = math.sqrt(images)
    one = sparse_update(w_one, g_one, mom_one, avg_one, mask_one, rank_one, 1.3 * root)
    bno = dense_update(
        first_norm_params,
        jnp.stack([first_norm_gain, first_shift_bias]),
        mom_bn_one,
        avg_bn_one,
        8.0 * root,
    )
    two = sparse_update(w_two, g_two, mom_two, avg_two, mask_two, rank_two, 0.25 * root)
    bnt = dense_update(
        second_norm_params,
        jnp.stack([second_norm_gain, second_shift_bias]),
        mom_bn_two,
        avg_bn_two,
        root,
    )
    top_head = dense_update(w_head, part_head, mom_head, avg_head, 40.0)
    return (
        loss,
        one[0],
        one[1],
        one[2],
        one[3],
        one[4],
        bno[0],
        bno[1],
        bno[2],
        two[0],
        two[1],
        two[2],
        two[3],
        two[4],
        bnt[0],
        bnt[1],
        bnt[2],
        top_head[0],
        top_head[1],
        top_head[2],
        top_head[0].astype(jnp.bfloat16),
    )


def solution(mesh):
    in_specs = (
        P("img", None, None),
        P(("img", "ch")),
        P(("img", "ch")),
        P("img", None),
        P(None, "ch"),
        P(None, "ch"),
        P(None, "ch"),
        P(None, "ch"),
        P(None, "ch"),
        P(None, "ch"),
        P(None, "ch"),
        P(None, "ch"),
        P(("img", "ch")),
        P(("img", "ch")),
        P(("img", "ch")),
        P(("img", "ch")),
        P(("img", "ch")),
        P(),
        P(),
        P(),
        P(("img", "ch")),
        P(("img", "ch")),
        P(("img", "ch")),
    )
    out_specs = (
        P(),
        P(None, "ch"),
        P(None, "ch"),
        P(None, "ch"),
        P(None, "ch"),
        P(None, "ch"),
        P(None, "ch"),
        P(None, "ch"),
        P(None, "ch"),
        P(("img", "ch")),
        P(("img", "ch")),
        P(("img", "ch")),
        P(("img", "ch")),
        P(("img", "ch")),
        P(),
        P(),
        P(),
        P(("img", "ch")),
        P(("img", "ch")),
        P(("img", "ch")),
        P(("img", "ch")),
    )
    return jax.shard_map(shards, mesh=mesh, in_specs=in_specs, out_specs=out_specs, check_vma=False)
```

profile of v0, /device:TPU:0, one launch (start us, length us, event | category | flops | bytes accessed | tf_op | source)
XLA Modules:
  0.0 576.8 jit_solution(3067732156576850317)
XLA Ops:
  7.2 1.7 multiply_convert_fusion.3
  9.0 0.7 convert_bitcast_fusion.1
  9.7 13.4 %all-gather = f32[8,8,2]{1,2,0:T(2,128)S(1)} all-gather(f32[1,8,2]{1,2,0:T(2,128)S(1)} %maximum_bitcast_fusion), channel_id=1, replica_groups=mesh['img'=4,'ch'=8] {'ch'}, dimensions={0}, use_global_device_ids=true | all-gather | bytes 576 | tf_op jit(solution)/shard_map/all_gather | solution.py:104
  23.2 0.6 slice_reduce_fusion
  23.8 9.1 %fusion.29 = (f32[64]{0:T(128)S(1)}, f32[64]{0:T(128)S(1)}, f32[64,3136]{1,0:T(8,128)S(1)}) fusion(bf16[3136,2048]{1,0:T(8,128)(2,1)} %bitcast.114, f32[2048,64]{0,1:T(8,128)} %param.27, s32[2048,64]{0,1:T(8,128)} %param.30), kind=kOutput, calls=%fused_computation.118 | convolution fusion | flops 823078784 | bytes 14696960 | tf_op jit(solution)/shard_map/dot_general | solution.py:116
  32.9 10.7 %all-reduce.16 = (f32[]{:T(128)}, f32[64]{0:T(128)S(1)}, f32[64]{0:T(128)S(1)}) all-reduce(f32[]{:T(128)} %slice_reduce_fusion, f32[64]{0:T(128)S(1)} %get-tuple-element.26, f32[64]{0:T(128)S(1)} %get-tuple-element.25), channel_id=1, replica_groups=mesh['img'=4,'ch'=8] {'img'}, use_global_device_ids=true, to_apply=%region_2.3 | all-reduce | flops 129 | bytes 1032 | tf_op jit(solution)/shard_map/psum | solution.py:117
  43.6 0.5 fusion.22
  44.7 0.5 reshape.196
  45.1 2.4 copy.93
  47.5 1.3 reshape.231
  48.8 3.5 all-to-all-start
  52.4 61.0 %all-gather.1 = bf16[32,1,16000]{2,1,0:T(2,128)(2,1)S(1)} all-gather(bf16[1,1,16000]{2,1,0:T(2,128)(2,1)S(1)} %reshape.227), channel_id=1, replica_groups=mesh['img'=4,'ch'=8] {'img','ch'}, dimensions={0}, use_global_device_ids=true | all-gather | bytes 1056000 | tf_op jit(solution)/shard_map/all_gather | solution.py:111
  113.4 7.2 %reduce.3 = bf16[32,16000]{1,0:T(8,128)(2,1)} reduce(bf16[32,1,16000]{2,1,0:T(2,128)(2,1)S(1)} %all-gather.1, bf16[]{:T(256)} %constant.97), dimensions={1}, to_apply=%all-gather.1.reduce_sub_computation | reduce | bytes 2048002 | tf_op jit(solution)/shard_map/all_gather | solution.py:111
  120.6 3.7 reshape.209
  124.5 1.7 reshape.232
  126.2 1.7 copy.95
  127.9 0.5 reshape.197
  128.4 0.5 reshape.202
  129.1 0.8 constant_dynamic-update-slice_fusion.8
  129.9 0.8 constant_dynamic-update-slice_fusion.7
  130.8 0.8 constant_dynamic-update-slice_fusion.6
  131.6 0.8 constant_dynamic-update-slice_fusion.5
  132.4 0.8 constant_dynamic-update-slice_fusion.4
  133.2 0.8 constant_dynamic-update-slice_fusion.3
  134.0 0.8 constant_dynamic-update-slice_fusion.2
  134.8 0.8 constant_dynamic-update-slice_fusion.1
  135.6 0.8 constant_dynamic-update-slice_fusion
  136.4 8.5 %reshape.207 = bf16[4608,512]{1,0:T(8,128)(2,1)} reshape(bf16[2359296]{0:T(1024)(128)(2,1)} %all-gather.4.cloned.1.call-done) | data formatting | bytes 9437184 | tf_op jit(solution)/shard_map/reshape | solution.py:112
  144.9 5.5 fusion.30
  150.4 39.6 %all-reduce.13 = (f32[512]{0:T(512)S(1)}, f32[512]{0:T(512)S(1)}) all-reduce(f32[512]{0:T(512)S(1)} %get-tuple-element.28, f32[512]{0:T(512)S(1)} %get-tuple-element.27), channel_id=1, replica_groups=mesh['img'=4,'ch'=8] {'img','ch'}, use_global_device_ids=true, to_apply=%region_10.11 | all-reduce | flops 1024 | bytes 8192 | tf_op jit(solution)/shard_map/psum | solution.py:145
  190.9 1.3 multiply_reduce_fusion.3
  192.2 1.0 convolution_multiply_fusion
  193.2 0.5 fusion.26
  193.7 39.7 %all-reduce.12 = (f32[]{:T(128)}, f32[512]{0:T(512)S(1)}, f32[512]{0:T(512)S(1)}) all-reduce(f32[]{:T(128)} %get-tuple-element.57, f32[512]{0:T(512)S(1)} %get-tuple-element.22, f32[512]{0:T(512)S(1)} %get-tuple-element.21), channel_id=1, replica_groups=mesh['img'=4,'ch'=8] {'img','ch'}, use_global_device_ids=true, to_apply=%region_16.17 | all-reduce | flops 1025 | bytes 8200 | tf_op jit(solution)/shard_map/psum | solution.py:175
  233.4 4.7 fusion.27
  238.1 0.9 fusion.34
  239.4 0.5 fusion.7
  239.9 1.0 copy.97
  240.9 2.9 reshape.233
  243.9 3.5 all-to-all-start.1
  247.4 8.0 %convolution_bitcast_fusion = f32[576,4,8,128]{3,2,1,0:T(8,128)} fusion(bf16[392,4608]{1,0:T(8,128)(2,1)} %constant_dynamic-update-slice_fusion, f32[392,512]{1,0:T(8,128)S(1)} %get-tuple-element.89, f32[512]{0:T(512)S(1)} %get-tuple-element.32, f32[512]{0:T(512)S(1)} %broadcast_multiply_fusion, f32[512]{0:T(512)S(1)} %copy-done.39, ...), kind=kOutput, calls=%fused_computation | convolution fusion | flops 1853300736 | bytes 13883392 | tf_op jit(solution)/shard_map/pk,pc->kc/dot_general | solution.py:68
  255.4 9.8 %copy.105 = f32[576,4,8,128]{3,1,2,0:T(4,128)} copy(f32[576,4,8,128]{3,2,1,0:T(8,128)} %convolution_bitcast_fusion) | data formatting | bytes 18874368
  265.1 3.2 reshape.234
  268.3 1.1 copy.98
  269.8 1.5 copy.99
  271.3 1.9 copy.100
  273.2 0.6 fusion.28
  273.8 10.4 %all-reduce.15 = (f32[64]{0:T(128)S(1)}, f32[64]{0:T(128)S(1)}) all-reduce(f32[64]{0:T(128)S(1)} %get-tuple-element.24, f32[64]{0:T(128)S(1)} %get-tuple-element.23), channel_id=1, replica_groups=mesh['img'=4,'ch'=8] {'img'}, use_global_device_ids=true, to_apply=%region_24.25 | all-reduce | flops 128 | bytes 1024 | tf_op jit(solution)/shard_map/psum | solution.py:207
  284.3 7.8 %fusion = bf16[2048,64]{0,1:T(8,128)(2,1)} fusion(bf16[3136,2048]{1,0:T(8,128)(2,1)} %bitcast.115, f32[3136,64]{0,1:T(8,128)S(1)} %get-tuple-element.56, f32[64,3136]{1,0:T(8,128)S(1)} %get-tuple-element.88, f32[64]{0:T(128)S(1)} %get-tuple-element.38, f32[64]{0:T(128)S(1)} %broadcast_multiply_fusion.2, f32[64]{0:T(128)S(1)} %copy-done.25, ...), kind=kOutput, calls=%fused_computation.2 | convolution fusion | flops 823820288 | bytes 14714112 | tf_op jit(solution)/shard_map/pk,pc->kc/dot_general | solution.py:68
  292.5 0.5 fusion.19
  293.0 3.2 reshape.222
  296.3 0.9 copy-done
  297.4 1.0 or_select_fusion
  298.4 0.8 or_select_fusion.1
  299.2 0.6 add_multiply_fusion.3
  299.9 0.6 add_multiply_fusion.4
  300.4 34.6 %all-reduce.20.cloned.1.call-done = bf16[2048,64]{0,1:T(8,128)(2,1)} async-done(((bf16[2048,64]{0,1:T(8,128)(2,1)}), bf16[2048,64]{0,1:T(8,128)(2,1)}) %all-reduce.20.cloned.1.call-update) | async-done | bytes 262160 | tf_op jit(solution)/shard_map/psum | solution.py:223
  335.1 2.1 fusion.33
  337.2 2.1 add_multiply_fusion
  339.2 223.9 %all-reduce.22.cloned.1.call-done = (f32[2359296]{0:T(1024)}, f32[512000]{0:T(1024)}) async-done(((f32[2359296]{0:T(1024)}, f32[512000]{0:T(1024)}), (f32[2359296]{0:T(1024)}, f32[512000]{0:T(1024)})) %all-reduce.22.cloned.1.call-update) | async-done | bytes 11485200
  563.1 1.9 fusion.32
  565.1 1.8 add_multiply_fusion.1
  566.9 1.6 fusion.31
  568.5 1.5 add_multiply_fusion.2
  (115 shorter events, 3.5 us)
Async XLA Ops:
  7.2 129.2 %all-gather.4.cloned.1.call-start = ((), (), s32[]{:S(2)}) async-start(), calls=%async_computation.2 | async-start | bytes 4866048 | tf_op jit(solution)/shard_map/all_gather | solution.py:110
  23.8 19.8 %copy-start.21 = (f32[2,64]{1,0:T(2,128)S(1)}, f32[2,64]{1,0:T(2,128)}, u32[]{:S(2)}) copy-start(f32[2,64]{1,0:T(2,128)} %param.32) | copy-start | bytes 1540
  32.9 19.4 %copy-start.10 = (f32[16000]{0:T(1024)S(1)}, f32[16000]{0:T(1024)}, u32[]{:S(2)}) copy-start(f32[16000]{0:T(1024)} %param.43) | copy-start | bytes 192004
  43.6 0.9 copy-start.26
  43.6 0.9 copy-start.28
  44.1 0.5 copy-start.13
  44.1 0.6 copy-start.15
  48.8 75.7 %all-to-all-start = ((bf16[8,2,12544]{2,1,0:T(2,128)(2,1)}), bf16[8,2,12544]{2,1,0:T(2,128)(2,1)S(1)}, u32[]{:S(2)}, u32[]{:S(2)}) async-start(bf16[8,2,12544]{2,1,0:T(2,128)(2,1)} %reshape.231), calls=%async_computation | async-start | bytes 802816 | tf_op jit(solution)/shard_map/all_to_all | solution.py:131
  52.4 71.9 %copy-start.42 = (s32[1,64]{1,0:T(1,128)S(1)}, s32[1,64]{1,0:T(1,128)}, u32[]{:S(2)}) copy-start(s32[1,64]{1,0:T(1,128)} %param.26) | copy-start | bytes 772
  52.4 72.1 %copy-start.11 = (f32[2,512]{1,0:T(2,128)S(1)}, f32[2,512]{1,0:T(2,128)}, u32[]{:S(2)}) copy-start(f32[2,512]{1,0:T(2,128)} %param.40) | copy-start | bytes 12292
  124.5 66.2 %copy-start.32 = (s32[8]{0:T(128)}, s32[8]{0:T(128)S(1)}, u32[]{:S(2)}) copy-start(s32[8]{0:T(128)S(1)} %convert_bitcast_fusion) | copy-start | bytes 100
  190.0 48.1 %copy-start.38 = (f32[512]{0:T(512)}, f32[512]{0:T(512)S(1)}, u32[]{:S(2)}) copy-start(f32[512]{0:T(512)S(1)} %get-tuple-element.78) | copy-start | bytes 6148
  190.7 2.6 copy-start.17
  190.9 2.8 copy-start.23
  192.2 1.5 copy-start.34
  233.4 4.7 copy-start.19
  233.4 14.0 %copy-start.36 = (f32[512]{0:T(512)}, f32[512]{0:T(512)S(1)}, u32[]{:S(2)}) copy-start(f32[512]{0:T(512)S(1)} %get-tuple-element.32) | copy-start | bytes 6148
  239.4 8.0 %copy-start.39 = (f32[512]{0:T(512)S(1)}, f32[512]{0:T(512)}, u32[]{:S(2)}) copy-start(f32[512]{0:T(512)} %copy-done.38) | copy-start | bytes 6148
  243.9 21.3 %all-to-all-start.1 = ((bf16[8,2,12544]{2,1,0:T(2,128)(2,1)}), bf16[8,2,12544]{2,1,0:T(2,128)(2,1)S(1)}, u32[]{:S(2)}, u32[]{:S(2)}) async-start(bf16[8,2,12544]{2,1,0:T(2,128)(2,1)} %reshape.233), calls=%async_computation.1 | async-start | bytes 802816 | tf_op jit(solution)/shard_map/all_to_all | solution.py:203
  247.3 87.8 %all-reduce.20.cloned.1.call-start = ((), (), s32[]{:S(2)}) async-start(), calls=%async_computation.3 | async-start | bytes 524288 | tf_op jit(solution)/shard_map/psum | solution.py:223
  269.4 3.8 copy-start.14
  269.4 3.8 copy-start.16
  269.4 3.8 copy-start.27
  269.5 3.8 copy-start.29
  269.8 14.4 %copy-start.25 = (f32[64]{0:T(128)S(1)}, f32[64]{0:T(128)}, u32[]{:S(2)}) copy-start(f32[64]{0:T(128)} %get-tuple-element.83) | copy-start | bytes 772
  284.2 8.2 %copy-start.18 = (f32[8]{0:T(128)S(1)}, f32[8]{0:T(128)}, u32[]{:S(2)}) copy-start(f32[8]{0:T(128)} %copy-done.17) | copy-start | bytes 100
  284.2 8.2 %copy-start.24 = (f32[8]{0:T(128)S(1)}, f32[8]{0:T(128)}, u32[]{:S(2)}) copy-start(f32[8]{0:T(128)} %copy-done.23) | copy-start | bytes 100
  284.2 8.2 %copy-start.33 = (s32[8]{0:T(128)S(1)}, s32[8]{0:T(128)}, u32[]{:S(2)}) copy-start(s32[8]{0:T(128)} %copy-done.32) | copy-start | bytes 100
  284.2 8.2 %copy-start.35 = (f32[8]{0:T(128)S(1)}, f32[8]{0:T(128)}, u32[]{:S(2)}) copy-start(f32[8]{0:T(128)} %copy-done.34) | copy-start | bytes 100
  292.1 271.0 %all-reduce.22.cloned.1.call-start = ((), (), s32[]{:S(2)}) async-start(), calls=%async_computation.4 | async-start | bytes 22970368
  296.2 1.0 copy-start
  296.2 1.2 copy-start.2
  296.2 2.2 copy-start.1
  296.2 2.2 copy-start.5
  296.2 3.0 copy-start.12
  296.2 3.0 copy-start.20
  296.2 3.0 copy-start.30
  296.2 3.0 copy-start.31
  296.2 3.0 copy-start.37
  296.2 3.6 copy-start.22
  296.3 3.6 copy-start.40
  296.3 3.6 copy-start.41
  296.3 38.8 %copy-start.4 = (f32[2048,64]{0,1:T(8,128)S(1)}, f32[2048,64]{0,1:T(8,128)}, u32[]{:S(2)}) copy-start(f32[2048,64]{0,1:T(8,128)} %param.27) | copy-start | bytes 1572868
  296.3 38.8 %copy-start.8 = (f32[2048,64]{0,1:T(8,128)S(1)}, f32[2048,64]{0,1:T(8,128)}, u32[]{:S(2)}) copy-start(f32[2048,64]{0,1:T(8,128)} %param.28) | copy-start | bytes 1572868
  297.4 265.7 %copy-start.7 = (f32[73728]{0:T(1024)S(1)}, f32[73728]{0:T(1024)}, u32[]{:S(2)}) copy-start(f32[73728]{0:T(1024)} %param.35) | copy-start | bytes 884740
  337.1 232.9 %copy-start.3 = (f32[2048,64]{0,1:T(8,128)}, f32[2048,64]{0,1:T(8,128)S(1)}, u32[]{:S(2)}) copy-start(f32[2048,64]{0,1:T(8,128)S(1)} %get-tuple-element.55) | copy-start | bytes 1572868
  565.1 5.0 copy-start.6
  568.5 1.5 copy-start.9
Sparse Core Ops, SparseCore 0:
  11.6 73.5 all-gather.3
  292.2 42.8 all-reduce.19
  342.6 220.4 all-reduce.21
where the time goes:
time: 582 us; the launch traced here: 577 us
  waiting for transfers between devices  259 us (45%)
  blocking collectives  175 us (30%)
  local copies, waits for them, and re-layouts  55.6 us (10%)
  matrix products  37 us (6%)
  other arithmetic  29.1 us (5%)
  between operations  14.7 us (3%)
  starting transfers between devices  7.28 us (1%)
    unnamed x4, waiting for transfers between devices  224 us
    all_gather x1, blocking collectives, shards(): lax.all_gather(w_head.astype(jnp.bfloat16), ('img', 'ch'), axis=0, tiled=...  61 us
    psum x1, blocking collectives, shards(): lax.psum((jnp.sum(second_output_gradient, axis=0), jnp.sum(second_output_...  39.7 us
    psum x1, blocking collectives, shards(): lax.psum((jnp.sum(second_conv_output, axis=0), jnp.sum(second_conv_output...  39.6 us
    psum x1, waiting for transfers between devices, shards(): lax.psum(contract_rows(rows, first_preact_gradient).astype(jnp.bfloat16),...  34.6 us
    unnamed x101, local copies, waits for them, and re-layouts  26.9 us
    dot_general x3, matrix products, contract_rows(): jnp.einsum('pk,pc->kc', left, right, preferred_element_type=jnp.float32)  16.3 us
    all_gather x1, blocking collectives, shards(): slot_info = lax.all_gather(slot_info, 'ch', axis=1, tiled=True)  13.4 us
  transfers between devices with their start and end apart: 5, of which 2 were waited for; matrix products, arithmetic and copies ran while one was open for 12% of the time, Pallas kernels for 0%

commit v1 on v0

--- a/solution.py
+++ b/solution.py
@@ -10,6 +10,12 @@
 GROW = 10
 EPS = 1e-05
 MOMENTUM = 0.5
+
+
+def gather_and_add(shard, axis):
+    terms = lax.all_gather(shard, axis, axis=0, tiled=False)
+    summed = terms.sum(axis=0)
+    return summed
 
 
 def advance(weight, grad, velocity, rate):
@@ -220,7 +226,7 @@
         first_norm_gain,
         first_element_count,
     ).astype(jnp.bfloat16)
-    g_filt = lax.psum(
+    g_filt = gather_and_add(
         contract_rows(rows, first_preact_gradient).astype(jnp.bfloat16), "img"
     ).astype(jnp.float32)
     g_one = g_filt * mask_one.astype(jnp.float32)

time: 582 us -> 557 us (0.957)
  waiting for transfers between devices: 259 us -> 218 us
  blocking collectives: 175 us -> 191 us
    psum x1 -> x0, waiting for transfers between devices: 34.6 us -> none  [shards(): lax.psum(contract_rows(rows, first_preact_gradient).astype(jnp.bfloat16),...]
    all_to_all x0 -> x1, blocking collectives: none -> 15.6 us  [shards(): lax.all_to_all(d_act_in, 'ch', split_axis=2, concat_axis=1, tiled=True)]
    unnamed x4, waiting for transfers between devices: 224 us -> 218 us
    unnamed x101 -> x123, local copies, waits for them, and re-layouts: 26.9 us -> 27.2 us
  transfers between devices with their start and end apart: 5 -> 4, of which waited for: 2 -> 1; matrix products, arithmetic and copies ran while one was open for 12% -> 13% of each run, Pallas kernels for 0% -> 0%
where the time goes in v1:
time: 557 us; the launch traced here: 552 us
  waiting for transfers between devices  218 us (39%)
  blocking collectives  191 us (34%)
  local copies, waits for them, and re-layouts  59.6 us (11%)
  matrix products  36.8 us (7%)
  other arithmetic  28.3 us (5%)
  between operations  14.6 us (3%)
    unnamed x4, waiting for transfers between devices  218 us
    all_gather x1, blocking collectives, shards(): lax.all_gather(w_head.astype(jnp.bfloat16), ('img', 'ch'), axis=0, tiled=...  60.9 us
    psum x1, blocking collectives, shards(): lax.psum((jnp.sum(second_conv_output, axis=0), jnp.sum(second_conv_output...  39.7 us
    psum x1, blocking collectives, shards(): lax.psum((jnp.sum(second_output_gradient, axis=0), jnp.sum(second_output_...  39.4 us
    unnamed x123, local copies, waits for them, and re-layouts  27.2 us
    dot_general x3, matrix products, contract_rows(): jnp.einsum('pk,pc->kc', left, right, preferred_element_type=jnp.float32)  16.1 us
    all_to_all x1, blocking collectives, shards(): lax.all_to_all(d_act_in, 'ch', split_axis=2, concat_axis=1, tiled=True)  15.6 us
    all_gather x1, blocking collectives, shards(): slot_info = lax.all_gather(slot_info, 'ch', axis=1, tiled=True)  13.4 us
  transfers between devices with their start and end apart: 4, of which 1 were waited for; matrix products, arithmetic and copies ran while one was open for 13% of the time, Pallas kernels for 0%

profile of v1, /device:TPU:0, one launch (start us, length us, event | category | flops | bytes accessed | tf_op | source)
XLA Modules:
  0.0 551.6 jit_solution(15930042460276161133)
XLA Ops:
  7.2 1.7 multiply_convert_fusion.3
  9.0 0.7 convert_bitcast_fusion.1
  9.7 13.4 %all-gather.1 = f32[8,8,2]{1,2,0:T(2,128)S(1)} all-gather(f32[1,8,2]{1,2,0:T(2,128)S(1)} %maximum_bitcast_fusion), channel_id=1, replica_groups=mesh['img'=4,'ch'=8] {'ch'}, dimensions={0}, use_global_device_ids=true | all-gather | bytes 576 | tf_op jit(solution)/shard_map/all_gather | solution.py:110
  23.2 0.6 slice_reduce_fusion
  23.8 9.1 %fusion.29 = (f32[64]{0:T(128)S(1)}, f32[64]{0:T(128)S(1)}, f32[64,3136]{1,0:T(8,128)S(1)}) fusion(bf16[3136,2048]{1,0:T(8,128)(2,1)} %bitcast.116, f32[2048,64]{0,1:T(8,128)} %param.27, s32[2048,64]{0,1:T(8,128)} %param.30), kind=kOutput, calls=%fused_computation.118 | convolution fusion | flops 823078784 | bytes 14696960 | tf_op jit(solution)/shard_map/dot_general | solution.py:122
  32.9 10.7 %all-reduce.16 = (f32[]{:T(128)}, f32[64]{0:T(128)S(1)}, f32[64]{0:T(128)S(1)}) all-reduce(f32[]{:T(128)} %slice_reduce_fusion, f32[64]{0:T(128)S(1)} %get-tuple-element.26, f32[64]{0:T(128)S(1)} %get-tuple-element.25), channel_id=1, replica_groups=mesh['img'=4,'ch'=8] {'img'}, use_global_device_ids=true, to_apply=%region_2.3 | all-reduce | flops 129 | bytes 1032 | tf_op jit(solution)/shard_map/psum | solution.py:123
  43.6 0.5 fusion.22
  45.1 2.4 copy.93
  47.5 1.3 reshape.232
  48.8 3.5 all-to-all-start
  52.4 60.9 %all-gather.2 = bf16[32,1,16000]{2,1,0:T(2,128)(2,1)S(1)} all-gather(bf16[1,1,16000]{2,1,0:T(2,128)(2,1)S(1)} %reshape.228), channel_id=1, replica_groups=mesh['img'=4,'ch'=8] {'img','ch'}, dimensions={0}, use_global_device_ids=true | all-gather | bytes 1056000 | tf_op jit(solution)/shard_map/all_gather | solution.py:117
  113.3 7.2 %reduce.4 = bf16[32,16000]{1,0:T(8,128)(2,1)} reduce(bf16[32,1,16000]{2,1,0:T(2,128)(2,1)S(1)} %all-gather.2, bf16[]{:T(256)} %constant.98), dimensions={1}, to_apply=%all-gather.2.reduce_sub_computation | reduce | bytes 2048002 | tf_op jit(solution)/shard_map/all_gather | solution.py:117
  120.5 3.6 reshape.209
  124.4 1.7 reshape.233
  126.1 1.7 copy.95
  129.0 0.8 constant_dynamic-update-slice_fusion.8
  129.8 0.8 constant_dynamic-update-slice_fusion.7
  130.6 0.8 constant_dynamic-update-slice_fusion.6
  131.4 0.8 constant_dynamic-update-slice_fusion.5
  132.2 0.8 constant_dynamic-update-slice_fusion.4
  133.0 0.8 constant_dynamic-update-slice_fusion.3
  133.9 0.8 constant_dynamic-update-slice_fusion.2
  134.7 0.8 constant_dynamic-update-slice_fusion.1
  135.5 0.8 constant_dynamic-update-slice_fusion
  136.3 8.5 %reshape.207 = bf16[4608,512]{1,0:T(8,128)(2,1)} reshape(bf16[2359296]{0:T(1024)(128)(2,1)} %all-gather.6.cloned.1.call-done) | data formatting | bytes 9437184 | tf_op jit(solution)/shard_map/reshape | solution.py:118
  144.8 5.5 fusion.30
  150.3 39.7 %all-reduce.13 = (f32[512]{0:T(512)S(1)}, f32[512]{0:T(512)S(1)}) all-reduce(f32[512]{0:T(512)S(1)} %get-tuple-element.28, f32[512]{0:T(512)S(1)} %get-tuple-element.27), channel_id=1, replica_groups=mesh['img'=4,'ch'=8] {'img','ch'}, use_global_device_ids=true, to_apply=%region_10.11 | all-reduce | flops 1024 | bytes 8192 | tf_op jit(solution)/shard_map/psum | solution.py:151
  190.9 1.3 multiply_reduce_fusion.3
  192.2 0.5 copy-done.40
  192.7 1.0 convolution_multiply_fusion
  194.2 39.4 %all-reduce.12 = (f32[]{:T(128)}, f32[512]{0:T(512)S(1)}, f32[512]{0:T(512)S(1)}) all-reduce(f32[]{:T(128)} %get-tuple-element.57, f32[512]{0:T(512)S(1)} %get-tuple-element.22, f32[512]{0:T(512)S(1)} %get-tuple-element.21), channel_id=1, replica_groups=mesh['img'=4,'ch'=8] {'img','ch'}, use_global_device_ids=true, to_apply=%region_16.17 | all-reduce | flops 1025 | bytes 8200 | tf_op jit(solution)/shard_map/psum | solution.py:181
  233.6 4.7 fusion.27
  238.3 0.9 fusion.34
  239.6 0.5 fusion.7
  240.2 1.0 copy.97
  241.1 2.1 reshape.234
  243.3 15.6 %all_to_all.24 = bf16[8,2,12544]{2,1,0:T(2,128)(2,1)S(1)} all-to-all(bf16[8,2,12544]{2,1,0:T(2,128)(2,1)S(1)} %reshape.234), channel_id=1, replica_groups=mesh['img'=4,'ch'=8] {'ch'}, dimensions={0} | all-to-all | bytes 802816 | tf_op jit(solution)/shard_map/all_to_all | solution.py:209
  258.9 3.2 reshape.235
  262.1 1.9 copy.98
  263.9 1.5 reshape.224
  265.4 1.5 copy.99
  267.0 1.9 copy.100
  268.9 0.6 fusion.28
  269.5 11.2 %all-reduce.15 = (f32[64]{0:T(128)S(1)}, f32[64]{0:T(128)S(1)}) all-reduce(f32[64]{0:T(128)S(1)} %get-tuple-element.24, f32[64]{0:T(128)S(1)} %get-tuple-element.23), channel_id=1, replica_groups=mesh['img'=4,'ch'=8] {'img'}, use_global_device_ids=true, to_apply=%region_24.25 | all-reduce | flops 128 | bytes 1024 | tf_op jit(solution)/shard_map/psum | solution.py:213
  280.8 0.5 copy-done.51
  281.3 7.8 %fusion = bf16[2048,64]{0,1:T(8,128)(2,1)} fusion(bf16[3136,2048]{1,0:T(8,128)(2,1)} %bitcast.117, f32[3136,64]{0,1:T(8,128)S(1)} %get-tuple-element.56, f32[64,3136]{1,0:T(8,128)S(1)} %get-tuple-element.88, f32[64]{0:T(128)S(1)} %get-tuple-element.38, f32[64]{0:T(128)S(1)} %broadcast_multiply_fusion.2, f32[64]{0:T(128)S(1)} %copy-done.31, ...), kind=kOutput, calls=%fused_computation.2 | convolution fusion | flops 823820288 | bytes 14714112 | tf_op jit(solution)/shard_map/pk,pc->kc/dot_general | solution.py:74
  289.2 7.8 %convolution_bitcast_fusion = f32[576,4,8,128]{3,2,1,0:T(8,128)} fusion(bf16[392,4608]{1,0:T(8,128)(2,1)} %constant_dynamic-update-slice_fusion, f32[392,512]{1,0:T(8,128)S(1)} %get-tuple-element.89, f32[512]{0:T(512)S(1)} %copy-done.43, f32[512]{0:T(512)S(1)} %copy-done.46, f32[512]{0:T(512)S(1)} %copy-done.48, f32[512]{0:T(512)S(1)} %get-tuple-element.79, ...), kind=kOutput, calls=%fused_computation | convolution fusion | flops 1853300736 | bytes 13883392 | tf_op jit(solution)/shard_map/pk,pc->kc/dot_general | solution.py:74
  297.0 9.8 %copy.105 = f32[576,4,8,128]{3,1,2,0:T(4,128)} copy(f32[576,4,8,128]{3,2,1,0:T(8,128)} %convolution_bitcast_fusion) | data formatting | bytes 18874368
  306.9 0.5 fusion.19
  307.4 3.3 reshape.222
  310.8 0.9 copy-done
  311.8 1.0 or_select_fusion
  312.8 0.8 or_select_fusion.1
  313.7 0.6 add_multiply_fusion.3
  314.3 0.6 add_multiply_fusion.4
  314.9 1.8 reshape.225
  316.8 2.2 reduce_sum.152
  319.0 2.3 fusion.33
  321.3 0.9 add_multiply_fusion
  322.1 217.7 %all-reduce.19.cloned.1.call-done = (f32[2359296]{0:T(1024)}, f32[512000]{0:T(1024)}) async-done(((f32[2359296]{0:T(1024)}, f32[512000]{0:T(1024)}), (f32[2359296]{0:T(1024)}, f32[512000]{0:T(1024)})) %all-reduce.19.cloned.1.call-update) | async-done | bytes 11485200
  539.9 1.9 fusion.32
  541.8 0.8 add_multiply_fusion.1
  542.6 1.6 fusion.31
  544.2 0.6 add_multiply_fusion.2
  (138 shorter events, 4.7 us)
Async XLA Ops:
  7.2 129.1 %all-gather.6.cloned.1.call-start = ((), (), s32[]{:S(2)}) async-start(), calls=%async_computation.2 | async-start | bytes 4866048 | tf_op jit(solution)/shard_map/all_gather | solution.py:116
  23.8 19.7 %copy-start.25 = (f32[2,64]{1,0:T(2,128)S(1)}, f32[2,64]{1,0:T(2,128)}, u32[]{:S(2)}) copy-start(f32[2,64]{1,0:T(2,128)} %param.32) | copy-start | bytes 1540
  32.9 19.4 %copy-start.11 = (f32[16000]{0:T(1024)S(1)}, f32[16000]{0:T(1024)}, u32[]{:S(2)}) copy-start(f32[16000]{0:T(1024)} %param.43) | copy-start | bytes 192004
  43.6 0.9 copy-start.32
  43.6 0.9 copy-start.34
  44.1 0.5 copy-start.17
  44.1 0.5 copy-start.19
  48.8 75.6 %all-to-all-start = ((bf16[8,2,12544]{2,1,0:T(2,128)(2,1)}), bf16[8,2,12544]{2,1,0:T(2,128)(2,1)S(1)}, u32[]{:S(2)}, u32[]{:S(2)}) async-start(bf16[8,2,12544]{2,1,0:T(2,128)(2,1)} %reshape.232), calls=%async_computation | async-start | bytes 802816 | tf_op jit(solution)/shard_map/all_to_all | solution.py:137
  52.2 262.7 %all-gather.8.cloned.1.call-start = ((), (), s32[]{:S(2)}) async-start(), calls=%async_computation.3 | async-start | bytes 1310720 | tf_op jit(solution)/shard_map/all_gather | solution.py:16
  52.4 71.8 %copy-start.53 = (s32[1,64]{1,0:T(1,128)S(1)}, s32[1,64]{1,0:T(1,128)}, u32[]{:S(2)}) copy-start(s32[1,64]{1,0:T(1,128)} %param.26) | copy-start | bytes 772
  52.4 72.0 %copy-start.15 = (f32[2,512]{1,0:T(2,128)S(1)}, f32[2,512]{1,0:T(2,128)}, u32[]{:S(2)}) copy-start(f32[2,512]{1,0:T(2,128)} %param.40) | copy-start | bytes 12292
  124.3 66.3 %copy-start.38 = (s32[8]{0:T(128)}, s32[8]{0:T(128)S(1)}, u32[]{:S(2)}) copy-start(s32[8]{0:T(128)S(1)} %convert_bitcast_fusion) | copy-start | bytes 100
  190.0 48.3 %copy-start.47 = (f32[512]{0:T(512)}, f32[512]{0:T(512)S(1)}, u32[]{:S(2)}) copy-start(f32[512]{0:T(512)S(1)} %get-tuple-element.78) | copy-start | bytes 6148
  190.6 47.7 %copy-start.21 = (f32[8]{0:T(128)}, f32[8]{0:T(128)S(1)}, u32[]{:S(2)}) copy-start(f32[8]{0:T(128)S(1)} %get-tuple-element.90) | copy-start | bytes 100
  190.9 1.3 copy-start.29
  192.2 0.5 copy-start.40
  233.6 4.7 copy-start.23
  233.6 4.8 copy-start.42
  233.6 4.8 copy-start.45
  263.9 5.0 copy-start.18
  263.9 5.0 copy-start.20
  263.9 5.0 copy-start.33
  263.9 5.0 copy-start.35
  265.4 15.8 %copy-start.31 = (f32[64]{0:T(128)S(1)}, f32[64]{0:T(128)}, u32[]{:S(2)}) copy-start(f32[64]{0:T(128)} %get-tuple-element.83) | copy-start | bytes 772
  280.7 0.5 copy-start.51
  280.7 8.4 %copy-start.27 = (f32[64]{0:T(128)}, f32[64]{0:T(128)S(1)}, u32[]{:S(2)}) copy-start(f32[64]{0:T(128)S(1)} %get-tuple-element.38) | copy-start | bytes 772
  281.3 7.9 %copy-start.43 = (f32[512]{0:T(512)S(1)}, f32[512]{0:T(512)}, u32[]{:S(2)}) copy-start(f32[512]{0:T(512)} %copy-done.42) | copy-start | bytes 6148
  281.3 7.9 %copy-start.46 = (f32[512]{0:T(512)S(1)}, f32[512]{0:T(512)}, u32[]{:S(2)}) copy-start(f32[512]{0:T(512)} %copy-done.45) | copy-start | bytes 6148
  281.3 8.0 %copy-start.48 = (f32[512]{0:T(512)S(1)}, f32[512]{0:T(512)}, u32[]{:S(2)}) copy-start(f32[512]{0:T(512)} %copy-done.47) | copy-start | bytes 6148
  289.1 250.7 %all-reduce.19.cloned.1.call-start = ((), (), s32[]{:S(2)}) async-start(), calls=%async_computation.4 | async-start | bytes 22970368
  297.0 9.9 %copy-start.22 = (f32[8]{0:T(128)S(1)}, f32[8]{0:T(128)}, u32[]{:S(2)}) copy-start(f32[8]{0:T(128)} %copy-done.21) | copy-start | bytes 100
  297.0 9.9 %copy-start.30 = (f32[8]{0:T(128)S(1)}, f32[8]{0:T(128)}, u32[]{:S(2)}) copy-start(f32[8]{0:T(128)} %copy-done.29) | copy-start | bytes 100
  297.0 9.9 %copy-start.39 = (s32[8]{0:T(128)S(1)}, s32[8]{0:T(128)}, u32[]{:S(2)}) copy-start(s32[8]{0:T(128)} %copy-done.38) | copy-start | bytes 100
  297.0 9.9 %copy-start.41 = (f32[8]{0:T(128)S(1)}, f32[8]{0:T(128)}, u32[]{:S(2)}) copy-start(f32[8]{0:T(128)} %copy-done.40) | copy-start | bytes 100
  310.6 1.0 copy-start
  310.6 1.2 copy-start.2
  310.6 2.2 copy-start.1
  310.6 2.2 copy-start.5
  310.6 3.0 copy-start.16
  310.7 3.0 copy-start.24
  310.7 3.0 copy-start.36
  310.7 3.0 copy-start.37
  310.7 3.0 copy-start.44
  310.7 3.6 copy-start.26
  310.7 3.6 copy-start.28
  310.7 3.6 copy-start.49
  310.7 3.6 copy-start.50
  310.8 3.6 copy-start.52
  310.8 8.2 %copy-start.4 = (f32[2048,64]{0,1:T(8,128)S(1)}, f32[2048,64]{0,1:T(8,128)}, u32[]{:S(2)}) copy-start(f32[2048,64]{0,1:T(8,128)} %param.27) | copy-start | bytes 1572868
  316.8 223.1 %copy-start.7 = (f32[73728]{0:T(1024)S(1)}, f32[73728]{0:T(1024)}, u32[]{:S(2)}) copy-start(f32[73728]{0:T(1024)} %param.35) | copy-start | bytes 884740
  319.0 2.3 copy-start.8
  321.2 223.6 %copy-start.3 = (f32[2048,64]{0,1:T(8,128)}, f32[2048,64]{0,1:T(8,128)S(1)}, u32[]{:S(2)}) copy-start(f32[2048,64]{0,1:T(8,128)S(1)} %get-tuple-element.55) | copy-start | bytes 1572868
  321.2 220.6 %copy-start.9 = (f32[73728]{0:T(1024)S(1)}, f32[73728]{0:T(1024)}, u32[]{:S(2)}) copy-start(f32[73728]{0:T(1024)} %param.37) | copy-start | bytes 884740
  321.2 221.4 %copy-start.12 = (f32[16000]{0:T(1024)S(1)}, f32[16000]{0:T(1024)}, u32[]{:S(2)}) copy-start(f32[16000]{0:T(1024)} %param.43) | copy-start | bytes 192004
  321.2 221.4 %copy-start.14 = (f32[16000]{0:T(1024)S(1)}, f32[16000]{0:T(1024)}, u32[]{:S(2)}) copy-start(f32[16000]{0:T(1024)} %param.44) | copy-start | bytes 192004
  321.3 223.0 %copy-start.13 = (f32[16000]{0:T(1024)S(1)}, f32[16000]{0:T(1024)}, u32[]{:S(2)}) copy-start(f32[16000]{0:T(1024)} %param.45) | copy-start | bytes 192004
  541.8 3.1 copy-start.6
  544.2 0.7 copy-start.10
Sparse Core Ops, SparseCore 0:
  11.6 73.5 all-gather.5
  289.3 23.6 all-gather.7
  319.4 220.4 all-reduce.18
